TPU v7x, 32 devices: a whole 2x2x4 slice. The times are simulated.
32 devices in a mesh: blk: 8 (over z, y), head: 4 (over x, core).
Axes of the slice: x: 2, y: 2, z: 4, core: 2. Of those that a mesh axis runs over, the one named last changes fastest.
Arguments:
- queries: bfloat16 [2048, 8192], P(('blk', 'head')), may hold values from -6 to 6
- keys: bfloat16 [2048, 1024], P(('blk', 'head')), may hold values from -6 to 6
- values: bfloat16 [2048, 1024], P(('blk', 'head')), may hold values from -6 to 6
- doc_lengths: int32 [6], replicated, may hold values from 1 to 1024, 2048 in all
- stored_block_order: int32 [16], replicated, may hold values from 0 to 15, each once
Outputs:
- attended: bfloat16 [2048, 8192], P(('blk', 'head'))
Inputs may be any that keep to these rules, and one draw needn't show every extreme that they name: `stored_block_order`: each stored block holds a different prompt block.
All inputs are finite; a program needn't handle non-finite values.
Results may differ from a plain program's by a relative error of at most 0.0034.
Values may be sent and summed in bfloat16 or wider, within the bound.
A program may use at most 64 MiB of HBM per device.

v0:
```python
import jax
import jax.numpy as jnp
from jax import lax
from jax.sharding import PartitionSpec as P

HEAD_WIDTH = 128


def passed_along(value, axis, steps):
    count = lax.axis_size(axis)
    pairs = [(source, (source + steps) % count) for source in range(count)]
    return lax.ppermute(value, axis, pairs)


def locate(start, count, stored_block_order, ends, block_length):
    block_count = stored_block_order.shape[0]
    idx = start + jnp.arange(count, dtype=jnp.int32)
    stored_slot = idx // block_length
    document_match = stored_slot[:, None] == jnp.arange(block_count, dtype=jnp.int32)[None, :]
    orig = (
        jnp.sum(jnp.where(document_match, stored_block_order[None, :], 0), axis=1) * block_length
        + idx % block_length
    )
    docs = jnp.sum((orig[:, None] >= ends[None, :]).astype(jnp.int32), axis=1)
    return (orig, docs)


def body(queries, keys, values, doc_lengths, stored_block_order):
    q_local, k_local, v_local = (
        lax.all_to_all(queries, "head", split_axis=1, concat_axis=0, tiled=True),
        lax.all_to_all(keys, "head", split_axis=1, concat_axis=0, tiled=True),
        lax.all_to_all(values, "head", split_axis=1, concat_axis=0, tiled=True),
    )
    rows = q_local.shape[0]
    nblk = lax.axis_size("blk")
    me = lax.axis_index("blk")
    groups = k_local.shape[1] // HEAD_WIDTH
    head_ratio = q_local.shape[1] // HEAD_WIDTH // groups
    block_length = rows * nblk // stored_block_order.shape[0]
    ends = jnp.cumsum(doc_lengths)
    q_heads = q_local.reshape(rows, groups, head_ratio, HEAD_WIDTH)
    q_orig, q_docs = locate(me * rows, rows, stored_block_order, ends, block_length)
    scale = HEAD_WIDTH ** (-0.5)

    def attend(carry, key_rows, value_rows, start):
        count = key_rows.shape[0]
        k_orig, k_docs = locate(start, count, stored_block_order, ends, block_length)
        allowed = (k_orig[None, :] <= q_orig[:, None]) & (k_docs[None, :] == q_docs[:, None])
        top, total, accum = carry
        k_heads = key_rows.reshape(count, groups, HEAD_WIDTH)
        v_heads = value_rows.reshape(count, groups, HEAD_WIDTH)
        scores = (
            jnp.einsum("qgrd,kgd->grqk", q_heads, k_heads, preferred_element_type=jnp.float32)
            * scale
        )
        scores = jnp.where(allowed, scores, -1e30)
        new_top = jnp.maximum(top, jnp.max(scores, axis=-1))
        weights = jnp.where(allowed, jnp.exp(scores - new_top[..., None]), 0.0)
        factor = jnp.exp(top - new_top)
        total = total * factor + jnp.sum(weights, axis=-1)
        update = jnp.einsum(
            "grqk,kgd->grqd",
            weights.astype(jnp.bfloat16),
            v_heads,
            preferred_element_type=jnp.float32,
        )
        accum = accum * factor[..., None] + update
        return (new_top, total, accum)

    start_top = jnp.full((groups, head_ratio, rows), -1e30, jnp.float32)
    start_total = jnp.zeros((groups, head_ratio, rows), jnp.float32)
    start_accum = jnp.zeros((groups, head_ratio, rows, HEAD_WIDTH), jnp.float32)
    carry = (start_top, start_total, start_accum)
    carry = attend(carry, k_local, v_local, me * rows)
    paired = jnp.stack([k_local, v_local])

    def cycle_step(step, state):
        inner, moving = state
        moving = passed_along(moving, "blk", 1)
        source = (me - step) % nblk
        inner = attend(inner, moving[0], moving[1], source * rows)
        return (inner, moving)

    carry, paired = lax.fori_loop(1, nblk, cycle_step, (carry, paired))
    top, total, accum = carry
    result = accum / total[..., None]
    result = (
        jnp.transpose(result, (2, 0, 1, 3))
        .reshape(rows, groups * head_ratio * HEAD_WIDTH)
        .astype(jnp.bfloat16)
    )
    return lax.all_to_all(result, "head", split_axis=0, concat_axis=1, tiled=True)


def solution(mesh):
    in_specs = (
        P(("blk", "head"), None),
        P(("blk", "head"), None),
        P(("blk", "head"), None),
        P(),
        P(),
    )
    out_specs = P(("blk", "head"), None)
    return jax.shard_map(body, mesh=mesh, in_specs=in_specs, out_specs=out_specs, check_vma=False)
```

profile of v0, /device:TPU:0, one launch (start us, length us, event | category | flops | bytes accessed | tf_op | source)
XLA Modules:
  0.0 160.4 jit_solution(8444719764753045083)
XLA Ops:
  0.0 1.6 copy.114
  1.6 4.2 %all-to-all-start = ((bf16[64,4,256]{2,0,1:T(8,128)(2,1)}), bf16[64,4,256]{2,0,1:T(8,128)(2,1)S(1)}, u32[]{:S(2)}, u32[]{:S(2)}) async-start(bf16[64,4,256]{2,0,1:T(8,128)(2,1)} %bitcast.72), calls=%async_computation | async-start | bytes 262144 | tf_op jit(solution)/shard_map/all_to_all | solution.py:31
  6.6 1.6 copy.113
  8.2 2.3 %copy.112 = bf16[8,4,8,2048]{3,2,0,1:T(8,128)(2,1)} copy(bf16[8,4,8,2048]{3,2,1,0:T(8,128)(2,1)} %bitcast.99) | data formatting | bytes 2097152 | tf_op jit(solution)/shard_map/all_to_all | solution.py:30
  10.5 3.3 %all-to-all-start.2 = ((bf16[64,4,256]{2,0,1:T(8,128)(2,1)}), bf16[64,4,256]{2,0,1:T(8,128)(2,1)S(1)}, u32[]{:S(2)}, u32[]{:S(2)}) async-start(bf16[64,4,256]{2,0,1:T(8,128)(2,1)} %bitcast.71), calls=%async_computation.2 | async-start | bytes 262144 | tf_op jit(solution)/shard_map/all_to_all | solution.py:32
  13.8 4.6 %all-to-all-done.2 = bf16[64,4,256]{2,0,1:T(8,128)(2,1)S(1)} async-done(((bf16[64,4,256]{2,0,1:T(8,128)(2,1)}), bf16[64,4,256]{2,0,1:T(8,128)(2,1)S(1)}, u32[]{:S(2)}, u32[]{:S(2)}) %all-to-all-start.2) | async-done | bytes 131104 | tf_op jit(solution)/shard_map/all_to_all | solution.py:32
  18.4 3.5 %all-to-all-start.1 = ((bf16[64,4,2048]{2,0,1:T(8,128)(2,1)}), bf16[64,4,2048]{2,0,1:T(8,128)(2,1)S(1)}, u32[]{:S(2)}, u32[]{:S(2)}) async-start(bf16[64,4,2048]{2,0,1:T(8,128)(2,1)} %bitcast.70), calls=%async_computation.1 | async-start | bytes 2097152 | tf_op jit(solution)/shard_map/all_to_all | solution.py:30
  23.3 13.1 %all-to-all-done.1 = bf16[64,4,2048]{2,0,1:T(8,128)(2,1)S(1)} async-done(((bf16[64,4,2048]{2,0,1:T(8,128)(2,1)}), bf16[64,4,2048]{2,0,1:T(8,128)(2,1)S(1)}, u32[]{:S(2)}, u32[]{:S(2)}) %all-to-all-start.1) | async-done | bytes 1048608 | tf_op jit(solution)/shard_map/all_to_all | solution.py:30
  37.9 1.0 fusion.19
  38.9 1.7 %fusion.27 = f32[2,8,256,128]{3,2,1,0:T(8,128)S(1)} fusion(f32[2,256,256,8]{2,1,3,0:T(8,128)S(1)} %get-tuple-element.398, f32[2,8,256]{2,1,0:T(8,128)S(1)} %broadcast_maximum_fusion, pred[256,256]{0,1:T(8,128)(4,1)S(1)} %compare_and_fusion.1, f32[2,8,256]{2,1,0:T(8,128)S(1)} %get-tuple-element.395, bf16[256,2,128,1]{2,1,0,3:T(2,128)(2,1)S(1)} %bitcast.103), kind=kOutput, calls=%fused_computation.42 | convolution fusion | flops 274202624 | bytes 6520832 | tf_op jit(solution)/shard_map/grqk,kgd->grqd/dot_general | solution.py:61
  40.6 99.9 %while.22 = (s32[]{:T(128)}, f32[2,8,256]{2,1,0:T(8,128)S(1)}, f32[2,8,256]{2,1,0:T(8,128)S(1)}, f32[2,8,256,128]{3,2,1,0:T(8,128)S(1)}, bf16[2,256,256]{1,2,0:T...) while((s32[]{:T(128)}, f32[2,8,256]{2,1,0:T(8,128)S(1)}, ...), condition=%wide.region_10.11_spmd, body=%wide.region_5.10_spmd.sunk | while | flops 551779840 | bytes 20721056 | solution.py:84
  40.6 2.1 %collective-permute-start = (bf16[2,256,256]{1,2,0:T(8,128)(2,1)}, bf16[2,256,256]{1,2,0:T(8,128)(2,1)S(1)}, u32[]{:S(2)}, u32[]{:S(2)}) collective-permute-start(bf16[2,256,256]{1,2,0:T(8,128)(2,1)} %get-tuple-element.498), channel_id=1, source_target_pairs={{0,4},{4,8},{8,12},{12,16},{16,20},{20,24},{24,28},{28,0},{1,5},{5... | collective-permute-start | bytes 786440 | tf_op jit(solution)/shard_map/while/body/eval_jaxpr/ppermute | solution.py:12
  43.1 9.0 %collective-permute-done = bf16[2,256,256]{1,2,0:T(8,128)(2,1)S(1)} collective-permute-done((bf16[2,256,256]{1,2,0:T(8,128)(2,1)}, bf16[2,256,256]{1,2,0:T(8,128)(2,1)S(1)}, u32[]{:S(2)}, u32[]{:S(2)}) %collective-permute-start) | collective-permute-done | bytes 262176 | tf_op jit(solution)/shard_map/while/body/eval_jaxpr/ppermute | solution.py:12
  53.0 1.0 fusion.60
  54.1 1.9 %multiply_add_fusion.5 = f32[2,8,256,128]{3,2,1,0:T(8,128)S(1)} fusion(f32[2,8,256,128]{3,2,1,0:T(8,128)S(1)} %get-tuple-element.497, bf16[256,2,128,1]{0,2,3,1:T(8,128)(2,1)S(1)} %bitcast.94, f32[2,256,256,8]{2,1,3,0:T(8,128)S(1)} %get-tuple-element.474, f32[2,8,256]{2,1,0:T(8,128)S(1)} %max.12, pred[256,256]{0,1:T(8,128)(4,1)S(1)} %compare_and_fusion.3, ...), kind=kOutput, calls=%fused_computation.6.clone.1 | convolution fusion | flops 274726912 | bytes 8617984 | tf_op jit(solution)/shard_map/while/body/eval_jaxpr/grqk,kgd->grqd/dot_general | solution.py:61
  57.0 9.8 %collective-permute-done = bf16[2,256,256]{1,2,0:T(8,128)(2,1)S(1)} collective-permute-done((bf16[2,256,256]{1,2,0:T(8,128)(2,1)}, bf16[2,256,256]{1,2,0:T(8,128)(2,1)S(1)}, u32[]{:S(2)}, u32[]{:S(2)}) %collective-permute-start) | collective-permute-done | bytes 262176 | tf_op jit(solution)/shard_map/while/body/eval_jaxpr/ppermute | solution.py:12
  67.8 1.0 fusion.60
  68.8 1.9 %multiply_add_fusion.5 = f32[2,8,256,128]{3,2,1,0:T(8,128)S(1)} fusion(f32[2,8,256,128]{3,2,1,0:T(8,128)S(1)} %get-tuple-element.497, bf16[256,2,128,1]{0,2,3,1:T(8,128)(2,1)S(1)} %bitcast.94, f32[2,256,256,8]{2,1,3,0:T(8,128)S(1)} %get-tuple-element.474, f32[2,8,256]{2,1,0:T(8,128)S(1)} %max.12, pred[256,256]{0,1:T(8,128)(4,1)S(1)} %compare_and_fusion.3, ...), kind=kOutput, calls=%fused_computation.6.clone.1 | convolution fusion | flops 274726912 | bytes 8617984 | tf_op jit(solution)/shard_map/while/body/eval_jaxpr/grqk,kgd->grqd/dot_general | solution.py:61
  71.8 8.9 %collective-permute-done = bf16[2,256,256]{1,2,0:T(8,128)(2,1)S(1)} collective-permute-done((bf16[2,256,256]{1,2,0:T(8,128)(2,1)}, bf16[2,256,256]{1,2,0:T(8,128)(2,1)S(1)}, u32[]{:S(2)}, u32[]{:S(2)}) %collective-permute-start) | collective-permute-done | bytes 262176 | tf_op jit(solution)/shard_map/while/body/eval_jaxpr/ppermute | solution.py:12
  81.6 1.0 fusion.60
  82.7 1.9 %multiply_add_fusion.5 = f32[2,8,256,128]{3,2,1,0:T(8,128)S(1)} fusion(f32[2,8,256,128]{3,2,1,0:T(8,128)S(1)} %get-tuple-element.497, bf16[256,2,128,1]{0,2,3,1:T(8,128)(2,1)S(1)} %bitcast.94, f32[2,256,256,8]{2,1,3,0:T(8,128)S(1)} %get-tuple-element.474, f32[2,8,256]{2,1,0:T(8,128)S(1)} %max.12, pred[256,256]{0,1:T(8,128)(4,1)S(1)} %compare_and_fusion.3, ...), kind=kOutput, calls=%fused_computation.6.clone.1 | convolution fusion | flops 274726912 | bytes 8617984 | tf_op jit(solution)/shard_map/while/body/eval_jaxpr/grqk,kgd->grqd/dot_general | solution.py:61
  85.6 8.9 %collective-permute-done = bf16[2,256,256]{1,2,0:T(8,128)(2,1)S(1)} collective-permute-done((bf16[2,256,256]{1,2,0:T(8,128)(2,1)}, bf16[2,256,256]{1,2,0:T(8,128)(2,1)S(1)}, u32[]{:S(2)}, u32[]{:S(2)}) %collective-permute-start) | collective-permute-done | bytes 262176 | tf_op jit(solution)/shard_map/while/body/eval_jaxpr/ppermute | solution.py:12
  95.4 1.0 fusion.60
  96.5 1.9 %multiply_add_fusion.5 = f32[2,8,256,128]{3,2,1,0:T(8,128)S(1)} fusion(f32[2,8,256,128]{3,2,1,0:T(8,128)S(1)} %get-tuple-element.497, bf16[256,2,128,1]{0,2,3,1:T(8,128)(2,1)S(1)} %bitcast.94, f32[2,256,256,8]{2,1,3,0:T(8,128)S(1)} %get-tuple-element.474, f32[2,8,256]{2,1,0:T(8,128)S(1)} %max.12, pred[256,256]{0,1:T(8,128)(4,1)S(1)} %compare_and_fusion.3, ...), kind=kOutput, calls=%fused_computation.6.clone.1 | convolution fusion | flops 274726912 | bytes 8617984 | tf_op jit(solution)/shard_map/while/body/eval_jaxpr/grqk,kgd->grqd/dot_general | solution.py:61
  99.4 8.9 %collective-permute-done = bf16[2,256,256]{1,2,0:T(8,128)(2,1)S(1)} collective-permute-done((bf16[2,256,256]{1,2,0:T(8,128)(2,1)}, bf16[2,256,256]{1,2,0:T(8,128)(2,1)S(1)}, u32[]{:S(2)}, u32[]{:S(2)}) %collective-permute-start) | collective-permute-done | bytes 262176 | tf_op jit(solution)/shard_map/while/body/eval_jaxpr/ppermute | solution.py:12
  110.3 1.9 %multiply_add_fusion.5 = f32[2,8,256,128]{3,2,1,0:T(8,128)S(1)} fusion(f32[2,8,256,128]{3,2,1,0:T(8,128)S(1)} %get-tuple-element.497, bf16[256,2,128,1]{0,2,3,1:T(8,128)(2,1)S(1)} %bitcast.94, f32[2,256,256,8]{2,1,3,0:T(8,128)S(1)} %get-tuple-element.474, f32[2,8,256]{2,1,0:T(8,128)S(1)} %max.12, pred[256,256]{0,1:T(8,128)(4,1)S(1)} %compare_and_fusion.3, ...), kind=kOutput, calls=%fused_computation.6.clone.1 | convolution fusion | flops 274726912 | bytes 8617984 | tf_op jit(solution)/shard_map/while/body/eval_jaxpr/grqk,kgd->grqd/dot_general | solution.py:61
  113.3 8.9 %collective-permute-done = bf16[2,256,256]{1,2,0:T(8,128)(2,1)S(1)} collective-permute-done((bf16[2,256,256]{1,2,0:T(8,128)(2,1)}, bf16[2,256,256]{1,2,0:T(8,128)(2,1)S(1)}, u32[]{:S(2)}, u32[]{:S(2)}) %collective-permute-start) | collective-permute-done | bytes 262176 | tf_op jit(solution)/shard_map/while/body/eval_jaxpr/ppermute | solution.py:12
  124.2 1.9 %multiply_add_fusion.5 = f32[2,8,256,128]{3,2,1,0:T(8,128)S(1)} fusion(f32[2,8,256,128]{3,2,1,0:T(8,128)S(1)} %get-tuple-element.497, bf16[256,2,128,1]{0,2,3,1:T(8,128)(2,1)S(1)} %bitcast.94, f32[2,256,256,8]{2,1,3,0:T(8,128)S(1)} %get-tuple-element.474, f32[2,8,256]{2,1,0:T(8,128)S(1)} %max.12, pred[256,256]{0,1:T(8,128)(4,1)S(1)} %compare_and_fusion.3, ...), kind=kOutput, calls=%fused_computation.6.clone.1 | convolution fusion | flops 274726912 | bytes 8617984 | tf_op jit(solution)/shard_map/while/body/eval_jaxpr/grqk,kgd->grqd/dot_general | solution.py:61
  127.1 8.9 %collective-permute-done = bf16[2,256,256]{1,2,0:T(8,128)(2,1)S(1)} collective-permute-done((bf16[2,256,256]{1,2,0:T(8,128)(2,1)}, bf16[2,256,256]{1,2,0:T(8,128)(2,1)S(1)}, u32[]{:S(2)}, u32[]{:S(2)}) %collective-permute-start) | collective-permute-done | bytes 262176 | tf_op jit(solution)/shard_map/while/body/eval_jaxpr/ppermute | solution.py:12
  138.0 1.9 %multiply_add_fusion.5 = f32[2,8,256,128]{3,2,1,0:T(8,128)S(1)} fusion(f32[2,8,256,128]{3,2,1,0:T(8,128)S(1)} %get-tuple-element.497, bf16[256,2,128,1]{0,2,3,1:T(8,128)(2,1)S(1)} %bitcast.94, f32[2,256,256,8]{2,1,3,0:T(8,128)S(1)} %get-tuple-element.474, f32[2,8,256]{2,1,0:T(8,128)S(1)} %max.12, pred[256,256]{0,1:T(8,128)(4,1)S(1)} %compare_and_fusion.3, ...), kind=kOutput, calls=%fused_computation.6.clone.1 | convolution fusion | flops 274726912 | bytes 8617984 | tf_op jit(solution)/shard_map/while/body/eval_jaxpr/grqk,kgd->grqd/dot_general | solution.py:61
  142.5 16.9 %all_to_all.64 = bf16[4,64,2048]{2,1,0:T(8,128)(2,1)S(1)} all-to-all(bf16[4,64,2048]{2,1,0:T(8,128)(2,1)S(1)} %convert_element_type.43), channel_id=1, replica_groups=mesh['blk'=8,'head'=4] {'head'}, dimensions={0} | all-to-all | bytes 2097152 | tf_op jit(solution)/shard_map/all_to_all | solution.py:92
  159.4 1.0 copy.97
  (107 shorter events, 22.1 us)
Async XLA Ops:
  0.0 22.0 %copy-start = (s32[16]{0:T(128)S(1)}, s32[16]{0:T(128)}, u32[]{:S(2)}) copy-start(s32[16]{0:T(128)} %param.11) | copy-start | bytes 196
  1.6 8.9 %all-to-all-start = ((bf16[64,4,256]{2,0,1:T(8,128)(2,1)}), bf16[64,4,256]{2,0,1:T(8,128)(2,1)S(1)}, u32[]{:S(2)}, u32[]{:S(2)}) async-start(bf16[64,4,256]{2,0,1:T(8,128)(2,1)} %bitcast.72), calls=%async_computation | async-start | bytes 262144 | tf_op jit(solution)/shard_map/all_to_all | solution.py:31
  10.5 8.0 %all-to-all-start.2 = ((bf16[64,4,256]{2,0,1:T(8,128)(2,1)}), bf16[64,4,256]{2,0,1:T(8,128)(2,1)S(1)}, u32[]{:S(2)}, u32[]{:S(2)}) async-start(bf16[64,4,256]{2,0,1:T(8,128)(2,1)} %bitcast.71), calls=%async_computation.2 | async-start | bytes 262144 | tf_op jit(solution)/shard_map/all_to_all | solution.py:32
  18.4 18.0 %all-to-all-start.1 = ((bf16[64,4,2048]{2,0,1:T(8,128)(2,1)}), bf16[64,4,2048]{2,0,1:T(8,128)(2,1)S(1)}, u32[]{:S(2)}, u32[]{:S(2)}) async-start(bf16[64,4,2048]{2,0,1:T(8,128)(2,1)} %bitcast.70), calls=%async_computation.1 | async-start | bytes 2097152 | tf_op jit(solution)/shard_map/all_to_all | solution.py:30
  40.6 11.5 %collective-permute-start = (bf16[2,256,256]{1,2,0:T(8,128)(2,1)}, bf16[2,256,256]{1,2,0:T(8,128)(2,1)S(1)}, u32[]{:S(2)}, u32[]{:S(2)}) collective-permute-start(bf16[2,256,256]{1,2,0:T(8,128)(2,1)} %get-tuple-element.498), channel_id=1, source_target_pairs={{0,4},{4,8},{8,12},{12,16},{16,20},{20,24},{24,28},{28,0},{1,5},{5... | collective-permute-start | bytes 786440 | tf_op jit(solution)/shard_map/while/body/eval_jaxpr/ppermute | solution.py:12
  56.7 10.2 %collective-permute-start = (bf16[2,256,256]{1,2,0:T(8,128)(2,1)}, bf16[2,256,256]{1,2,0:T(8,128)(2,1)S(1)}, u32[]{:S(2)}, u32[]{:S(2)}) collective-permute-start(bf16[2,256,256]{1,2,0:T(8,128)(2,1)} %get-tuple-element.498), channel_id=1, source_target_pairs={{0,4},{4,8},{8,12},{12,16},{16,20},{20,24},{24,28},{28,0},{1,5},{5... | collective-permute-start | bytes 786440 | tf_op jit(solution)/shard_map/while/body/eval_jaxpr/ppermute | solution.py:12
  71.4 9.3 %collective-permute-start = (bf16[2,256,256]{1,2,0:T(8,128)(2,1)}, bf16[2,256,256]{1,2,0:T(8,128)(2,1)S(1)}, u32[]{:S(2)}, u32[]{:S(2)}) collective-permute-start(bf16[2,256,256]{1,2,0:T(8,128)(2,1)} %get-tuple-element.498), channel_id=1, source_target_pairs={{0,4},{4,8},{8,12},{12,16},{16,20},{20,24},{24,28},{28,0},{1,5},{5... | collective-permute-start | bytes 786440 | tf_op jit(solution)/shard_map/while/body/eval_jaxpr/ppermute | solution.py:12
  85.2 9.3 %collective-permute-start = (bf16[2,256,256]{1,2,0:T(8,128)(2,1)}, bf16[2,256,256]{1,2,0:T(8,128)(2,1)S(1)}, u32[]{:S(2)}, u32[]{:S(2)}) collective-permute-start(bf16[2,256,256]{1,2,0:T(8,128)(2,1)} %get-tuple-element.498), channel_id=1, source_target_pairs={{0,4},{4,8},{8,12},{12,16},{16,20},{20,24},{24,28},{28,0},{1,5},{5... | collective-permute-start | bytes 786440 | tf_op jit(solution)/shard_map/while/body/eval_jaxpr/ppermute | solution.py:12
  99.1 9.3 %collective-permute-start = (bf16[2,256,256]{1,2,0:T(8,128)(2,1)}, bf16[2,256,256]{1,2,0:T(8,128)(2,1)S(1)}, u32[]{:S(2)}, u32[]{:S(2)}) collective-permute-start(bf16[2,256,256]{1,2,0:T(8,128)(2,1)} %get-tuple-element.498), channel_id=1, source_target_pairs={{0,4},{4,8},{8,12},{12,16},{16,20},{20,24},{24,28},{28,0},{1,5},{5... | collective-permute-start | bytes 786440 | tf_op jit(solution)/shard_map/while/body/eval_jaxpr/ppermute | solution.py:12
  112.9 9.3 %collective-permute-start = (bf16[2,256,256]{1,2,0:T(8,128)(2,1)}, bf16[2,256,256]{1,2,0:T(8,128)(2,1)S(1)}, u32[]{:S(2)}, u32[]{:S(2)}) collective-permute-start(bf16[2,256,256]{1,2,0:T(8,128)(2,1)} %get-tuple-element.498), channel_id=1, source_target_pairs={{0,4},{4,8},{8,12},{12,16},{16,20},{20,24},{24,28},{28,0},{1,5},{5... | collective-permute-start | bytes 786440 | tf_op jit(solution)/shard_map/while/body/eval_jaxpr/ppermute | solution.py:12
  126.8 9.3 %collective-permute-start = (bf16[2,256,256]{1,2,0:T(8,128)(2,1)}, bf16[2,256,256]{1,2,0:T(8,128)(2,1)S(1)}, u32[]{:S(2)}, u32[]{:S(2)}) collective-permute-start(bf16[2,256,256]{1,2,0:T(8,128)(2,1)} %get-tuple-element.498), channel_id=1, source_target_pairs={{0,4},{4,8},{8,12},{12,16},{16,20},{20,24},{24,28},{28,0},{1,5},{5... | collective-permute-start | bytes 786440 | tf_op jit(solution)/shard_map/while/body/eval_jaxpr/ppermute | solution.py:12
where the time goes:
time: 161 us; the launch traced here: 160 us
  waiting for transfers between devices  81.2 us (50%)
  matrix products  21.9 us (14%)
  blocking collectives  16.9 us (10%)
  local copies, waits for them, and re-layouts  14 us (9%)
  starting transfers between devices  13.2 us (8%)
  other arithmetic  12.6 us (8%)
    ppermute x7, waiting for transfers between devices, passed_along(): return lax.ppermute(value, axis, pairs)  63.5 us
    all_to_all x1, blocking collectives, body(): lax.all_to_all(result, 'head', split_axis=0, concat_axis=1, tiled=True)  16.9 us
    dot_general x8, matrix products, attend(): jnp.einsum('grqk,kgd->grqd', weights.astype(jnp.bfloat16), v_heads, prefe...  14.9 us
    all_to_all x1, waiting for transfers between devices, body(): lax.all_to_all(queries, 'head', split_axis=1, concat_axis=0, tiled=True)  13.1 us
    reduce_sum x8, other arithmetic, attend(): total = total * factor + jnp.sum(weights, axis=-1)  8.16 us
    dot_general x8, matrix products, attend(): jnp.einsum('qgrd,kgd->grqk', q_heads, k_heads, preferred_element_type=jnp...  7.01 us
    while x14, local copies, waits for them, and re-layouts  4.87 us
    all_to_all x1, waiting for transfers between devices, body(): lax.all_to_all(values, 'head', split_axis=1, concat_axis=0, tiled=True)  4.61 us
  transfers between devices with their start and end apart: 10, of which 9 were waited for; matrix products, arithmetic and copies ran while one was open for 5% of the time, Pallas kernels for 0%

commit v1 on v0

v1 whole, which is shorter than its diff:
```python
import functools
import math

import jax
import jax.numpy as jnp
from jax import lax
from jax.experimental import pallas as pl
from jax.experimental.pallas import tpu as pltpu
from jax.sharding import PartitionSpec as P

HEAD_WIDTH = 128
LANES = 128
SCORE_TO_LOG2 = HEAD_WIDTH ** (-0.5) * math.log2(math.e)
MASKED = -1e30
START_TOP = -1e25
F32 = jnp.float32
BF16 = jnp.bfloat16
MESH = pl.DeviceIdType.MESH


def query_limits(lengths_ref, order_ref, first_row, rows, block_length):
    lane = lax.broadcasted_iota(jnp.int32, (1, LANES), 1) % rows
    slot = first_row // block_length
    pos = order_ref[slot] * block_length + first_row % block_length + lane
    begin = jnp.zeros_like(pos)
    end = jnp.int32(0)
    for i in range(lengths_ref.shape[0]):
        end = end + lengths_ref[i]
        begin = jnp.where(pos >= end, end, begin)
    return pos, begin


def fill_bias(bias_ref, order_ref, first_slot, pos, begin, block_length):
    for j in range(bias_ref.shape[0] // block_length):
        key = (
            order_ref[first_slot + j] * block_length
            + lax.broadcasted_iota(jnp.int32, (block_length, LANES), 0)
        )
        allowed = (key <= pos) & (key >= begin)
        bias_ref[j * block_length : (j + 1) * block_length, :] = jnp.where(
            allowed, 0.0, MASKED
        ).astype(F32)


def stack_queries(g, q_ref, qt_ref, ratio):
    heads = [
        q_ref[:, pl.ds(pl.multiple_of((g * ratio + j) * HEAD_WIDTH, HEAD_WIDTH), HEAD_WIDTH)]
        for j in range(ratio)
    ]
    qt_ref[g] = jnp.concatenate(heads, axis=0).T


def attend(g, k, v, qt_ref, bias_ref, top_ref, total_ref, accum_ref):
    width = qt_ref.shape[2]
    scores = jnp.dot(k, qt_ref[g], preferred_element_type=F32)
    scores = scores + jnp.concatenate([bias_ref[...]] * (width // LANES), axis=1)
    top = top_ref[g]
    new_top = jnp.maximum(top, jnp.max(scores, axis=0, keepdims=True))
    weights = jnp.exp2((scores - new_top) * SCORE_TO_LOG2)
    factor = jnp.exp2((top - new_top) * SCORE_TO_LOG2)
    top_ref[g] = new_top
    total_ref[g] = total_ref[g] * factor + jnp.sum(weights, axis=0, keepdims=True)
    accum_ref[g] = accum_ref[g] * factor + jnp.dot(
        v.T, weights.astype(BF16), preferred_element_type=F32
    )


def finish(g, out_ref, total_ref, accum_ref, rows, ratio):
    result = (accum_ref[g] / total_ref[g]).T.astype(BF16)
    for j in range(ratio):
        cols = pl.ds(pl.multiple_of((g * ratio + j) * HEAD_WIDTH, HEAD_WIDTH), HEAD_WIDTH)
        out_ref[:, cols] = result[j * rows : (j + 1) * rows]


def reset(top_ref, total_ref, accum_ref):
    top_ref[...] = jnp.full(top_ref.shape, START_TOP, F32)
    total_ref[...] = jnp.zeros(total_ref.shape, F32)
    accum_ref[...] = jnp.zeros(accum_ref.shape, F32)


def head_columns(g):
    return pl.ds(pl.multiple_of(g * HEAD_WIDTH, HEAD_WIDTH), HEAD_WIDTH)


def chunk_kernel(ratio, block_length, first_ref, lengths_ref, order_ref, q_ref, k_ref, v_ref,
                 out_ref, qt_ref, bias_ref, top_ref, total_ref, accum_ref):
    step = pl.program_id(0)
    rows = q_ref.shape[0]
    groups = k_ref.shape[1] // HEAD_WIDTH
    chunk = k_ref.shape[0]

    @pl.when(step == 0)
    def _():
        reset(top_ref, total_ref, accum_ref)
        pl.loop(0, groups)(lambda g: stack_queries(g, q_ref, qt_ref, ratio))

    pos, begin = query_limits(lengths_ref, order_ref, first_ref[0], rows, block_length)
    fill_bias(bias_ref, order_ref, step * (chunk // block_length), pos, begin, block_length)

    @pl.loop(0, groups)
    def _(g):
        attend(g, k_ref[:, head_columns(g)], v_ref[:, head_columns(g)],
               qt_ref, bias_ref, top_ref, total_ref, accum_ref)

    @pl.when(step == pl.num_programs(0) - 1)
    def _():
        pl.loop(0, groups)(lambda g: finish(g, out_ref, total_ref, accum_ref, rows, ratio))


def gather_kernel(ratio, block_length, lengths_ref, order_ref, q_hbm, k_hbm, v_hbm, out_ref,
                  q_ref, k_buf, v_buf, qt_ref, bias_ref, top_ref, total_ref, accum_ref,
                  local_sem, k_recv, v_recv, k_send, v_send):
    rows, width = k_hbm.shape
    groups = width // HEAD_WIDTH
    blk, head = lax.axis_index("blk"), lax.axis_index("head")
    z, y, x, c = blk // 2, blk % 2, head // 2, head % 2
    me = blk * 4 + head
    hi = z // 2
    zz = z + hi * (3 - 2 * z)

    def flip(f):
        return f + hi * (3 - 2 * f)

    def plane(i):
        return flip(i + zz * (1 - 2 * i)) if i < 2 else flip(i)

    def shard(p, dy, dx, dc=0):
        yy = y + dy * (1 - 2 * y)
        xx = x + dx * (1 - 2 * x)
        cc = c + dc * (1 - 2 * c)
        return ((p * 2 + yy) * 2 + xx) * 2 + cc

    sibling = (blk, x * 2 + (1 - c))
    x_side = (blk, (1 - x) * 2 + c)
    y_side = (z * 2 + (1 - y), head)

    def z_side(f):
        return (flip(f) * 2 + y, head)

    barrier = pltpu.get_barrier_semaphore()
    for device in (sibling, x_side, y_side):
        pl.semaphore_signal(barrier, inc=1, device_id=device, device_id_type=MESH)

    @pl.when(zz == 0)
    def _():
        pl.semaphore_signal(barrier, inc=1, device_id=z_side(1), device_id_type=MESH)

    @pl.when(zz == 1)
    def _():
        for f in (0, 2):
            pl.semaphore_signal(barrier, inc=1, device_id=z_side(f), device_id_type=MESH)

    own_q = pltpu.make_async_copy(q_hbm, q_ref, local_sem.at[0])
    own_k = pltpu.make_async_copy(k_hbm, k_buf.at[me], local_sem.at[1])
    own_v = pltpu.make_async_copy(v_hbm, v_buf.at[me], local_sem.at[2])
    own_k.start()
    own_v.start()
    own_q.start()
    pl.semaphore_wait(barrier, 4 + zz)

    K = (k_hbm, k_buf, k_recv, k_send)
    V = (v_hbm, v_buf, v_recv, v_send)
    SIB, XS, YS, ZU, ZD = range(5)

    def copy(which, d, way, device, own=False):
        source, buf, recv, send = which
        return pltpu.make_async_remote_copy(
            src_ref=source if own else buf.at[d], dst_ref=buf.at[d],
            send_sem=send.at[way, d // 2], recv_sem=recv.at[d],
            device_id=device, device_id_type=MESH)

    def arrived(which, d):
        copy(which, d, SIB, sibling).wait_recv()

    def up_down(which, i, d, wait=False):
        def go(way, f):
            one = copy(which, d, way, z_side(f), own=i == 0)
            one.wait_send() if wait else one.start()

        if i == 0:
            @pl.when(zz == 0)
            def _():
                go(ZU, 1)

        @pl.when(zz == 1)
        def _():
            if i == 0:
                go(ZU, 2)
                go(ZD, 0)
            else:
                go(ZU if i == 1 else ZD, 2 if i == 1 else 0)

    def first(i):
        p = plane(i)
        a = shard(p, 0, 0)
        own = i == 0
        if not own:
            arrived(K, a)
        copy(K, a, YS, y_side, own).start()
        up_down(K, i, a)
        if not own:
            arrived(V, a)
        copy(V, a, XS, x_side, own).start()
        up_down(V, i, a)
        copy(K, a, XS, x_side, own).start()
        copy(V, a, YS, y_side, own).start()
        copy(K, a, SIB, sibling, own).start()
        copy(V, a, SIB, sibling, own).start()

    def second(i):
        p = plane(i)
        b, d = shard(p, 1, 0), shard(p, 0, 1)
        arrived(K, b)
        copy(K, b, XS, x_side).start()
        arrived(V, d)
        copy(V, d, YS, y_side).start()
        copy(K, b, SIB, sibling).start()
        copy(V, d, SIB, sibling).start()

    def third(i):
        p = plane(i)
        k_d, v_d = shard(p, 0, 1), shard(p, 1, 0)
        arrived(K, k_d)
        copy(K, k_d, SIB, sibling).start()
        arrived(V, v_d)
        copy(V, v_d, SIB, sibling).start()

    def fourth(i):
        p = plane(i)
        d = shard(p, 1, 1)
        arrived(K, d)
        copy(K, d, SIB, sibling).start()
        arrived(V, d)
        copy(V, d, SIB, sibling).start()

    def from_sibling(i):
        p = plane(i)
        for dy, dx in ((0, 0), (1, 0), (0, 1), (1, 1)):
            arrived(K, shard(p, dy, dx, 1))
            arrived(V, shard(p, dy, dx, 1))

    pos, begin = query_limits(lengths_ref, order_ref, me * rows, rows, block_length)
    slots = 8 * rows // block_length

    def prepare(i):
        fill_bias(bias_ref, order_ref, plane(i) * slots, pos, begin, block_length)

    def compute(i, lo, hi_):
        p = plane(i)

        @pl.loop(lo, hi_)
        def _(g):
            k = k_buf[pl.ds(p * 8, 8), :, head_columns(g)].reshape(8 * rows, HEAD_WIDTH)
            v = v_buf[pl.ds(p * 8, 8), :, head_columns(g)].reshape(8 * rows, HEAD_WIDTH)
            attend(g, k, v, qt_ref, bias_ref, top_ref, total_ref, accum_ref)
            if i == 3:
                finish(g, out_ref, total_ref, accum_ref, rows, ratio)

    first(0)
    reset(top_ref, total_ref, accum_ref)
    own_q.wait()
    pl.loop(0, groups)(lambda g: stack_queries(g, q_ref, qt_ref, ratio))
    second(0)
    first(1)
    third(0)
    fourth(0)
    own_k.wait()
    own_v.wait()
    for i in range(4):
        from_sibling(i)
        prepare(i)
        if i < 3:
            compute(i, 0, 2)
            second(i + 1)
            compute(i, 2, 4)
            if i < 2:
                first(i + 2)
            third(i + 1)
            compute(i, 4, groups)
            fourth(i + 1)
        else:
            compute(i, 0, groups)

    for i in range(4):
        p = plane(i)
        a, b, d, e = shard(p, 0, 0), shard(p, 1, 0), shard(p, 0, 1), shard(p, 1, 1)
        for which, extra in ((K, (b, XS, x_side)), (V, (d, YS, y_side))):
            copy(which, a, XS, x_side).wait_send()
            copy(which, a, YS, y_side).wait_send()
            copy(which, *extra).wait_send()
            up_down(which, i, a, wait=True)
            for s in (a, b, d, e):
                copy(which, s, SIB, sibling).wait_send()


def body(relayed, queries, keys, values, doc_lengths, stored_block_order):
    rows = queries.shape[0]
    groups = keys.shape[1] // HEAD_WIDTH
    ratio = queries.shape[1] // keys.shape[1]
    devices = lax.axis_size("blk") * lax.axis_size("head")
    block_length = rows * devices // stored_block_order.shape[0]
    chunk = max(512, block_length)
    scratch = [
        pltpu.VMEM((groups, HEAD_WIDTH, ratio * rows), BF16),
        pltpu.VMEM((chunk, LANES), F32),
        pltpu.VMEM((groups, 1, ratio * rows), F32),
        pltpu.VMEM((groups, 1, ratio * rows), F32),
        pltpu.VMEM((groups, HEAD_WIDTH, ratio * rows), F32),
    ]
    smem = pl.BlockSpec(memory_space=pltpu.SMEM)
    out_shape = jax.ShapeDtypeStruct(queries.shape, BF16)
    if relayed:
        gathered = pltpu.VMEM((devices, rows, keys.shape[1]), BF16)
        return pl.pallas_call(
            functools.partial(gather_kernel, ratio, block_length),
            out_shape=out_shape,
            in_specs=[smem, smem] + [pl.BlockSpec(memory_space=pl.ANY)] * 3,
            out_specs=pl.BlockSpec(memory_space=pltpu.VMEM),
            scratch_shapes=[pltpu.VMEM(queries.shape, BF16), gathered, gathered] + scratch + [
                pltpu.SemaphoreType.DMA((3,)),
                pltpu.SemaphoreType.DMA((devices,)),
                pltpu.SemaphoreType.DMA((devices,)),
                pltpu.SemaphoreType.DMA((5, devices // 2)),
                pltpu.SemaphoreType.DMA((5, devices // 2)),
            ],
            compiler_params=pltpu.CompilerParams(
                collective_id=0, has_side_effects=True, vmem_limit_bytes=48 << 20),
        )(doc_lengths, stored_block_order, queries, keys, values)
    keys = lax.all_gather(keys, ("blk", "head"), axis=0, tiled=True)
    values = lax.all_gather(values, ("blk", "head"), axis=0, tiled=True)
    first_row = (lax.axis_index("blk") * lax.axis_size("head") + lax.axis_index("head")) * rows
    whole = pl.BlockSpec(queries.shape, lambda i: (0, 0))
    part = pl.BlockSpec((chunk, keys.shape[1]), lambda i: (i, 0))
    return pl.pallas_call(
        functools.partial(chunk_kernel, ratio, block_length),
        out_shape=out_shape,
        grid=(keys.shape[0] // chunk,),
        in_specs=[smem, smem, smem, whole, part, part],
        out_specs=whole,
        scratch_shapes=scratch,
        compiler_params=pltpu.CompilerParams(vmem_limit_bytes=48 << 20),
    )(first_row.reshape(1), doc_lengths, stored_block_order, queries, keys, values)


def solution(mesh):
    rows = P(("blk", "head"), None)
    relayed = mesh.shape["blk"] == 8 and mesh.shape["head"] == 4
    return jax.shard_map(
        functools.partial(body, relayed), mesh=mesh,
        in_specs=(rows, rows, rows, P(), P()), out_specs=rows, check_vma=False)
```

time: 161 us -> 61.9 us (0.38)
  waiting for transfers between devices: 81.2 us -> 0 us
  Pallas kernels: 0 us -> 56.3 us
  matrix products: 21.9 us -> 0 us
  blocking collectives: 16.9 us -> 0 us
  starting transfers between devices: 13.2 us -> 0 us
  other arithmetic: 12.6 us -> 0 us
  local copies, waits for them, and re-layouts: 14 us -> 5.31 us
    ppermute x7 -> x0, waiting for transfers between devices: 63.5 us -> none  [passed_along(): return lax.ppermute(value, axis, pairs)]
    pallas_call x0 -> x1, Pallas kernels: none -> 56.3 us  [body(): pl.pallas_call(functools.partial(gather_kernel, ratio, block_length), out...]
    dot_general x16 -> x0, matrix products: 21.9 us -> none  [the longest x8 14.9 us: attend(): jnp.einsum('grqk,kgd->grqd', weights.astype(jnp.bfloat16), v_heads, prefe...]
    all_to_all x3 -> x0, waiting for transfers between devices: 17.8 us -> none  [the longest x1 13.1 us: body(): lax.all_to_all(queries, 'head', split_axis=1, concat_axis=0, tiled=True)]
    all_to_all x1 -> x0, blocking collectives: 16.9 us -> none  [body(): lax.all_to_all(result, 'head', split_axis=0, concat_axis=1, tiled=True)]
    all_to_all x3 -> x0, starting transfers between devices: 11.1 us -> none  [the longest x1 4.21 us: body(): lax.all_to_all(keys, 'head', split_axis=1, concat_axis=0, tiled=True)]
    reduce_sum x24 -> x0, other arithmetic: 9.57 us -> none  [the longest x8 8.16 us: attend(): total = total * factor + jnp.sum(weights, axis=-1)]
    all_to_all x4 -> x0, local copies, waits for them, and re-layouts: 6.47 us -> none  [the longest x1 2.3 us: body(): lax.all_to_all(queries, 'head', split_axis=1, concat_axis=0, tiled=True)]
  transfers between devices with their start and end apart: 10 -> 0, of which waited for: 9 -> 0; matrix products, arithmetic and copies ran while one was open for 5% -> 0% of each run, Pallas kernels for 0% -> 0%
where the time goes in v1:
time: 61.9 us; the launch traced here: 61.7 us
  Pallas kernels  56.3 us (91%)
  local copies, waits for them, and re-layouts  5.31 us (9%)
    pallas_call x1, Pallas kernels, body(): pl.pallas_call(functools.partial(gather_kernel, ratio, block_length), out...  56.3 us
    unnamed x11, local copies, waits for them, and re-layouts  5.31 us

profile of v1, /device:TPU:0, one launch (start us, length us, event | category | flops | bytes accessed | tf_op | source)
XLA Modules:
  0.0 61.7 jit_solution(7436807257636617673)
XLA Ops:
  0.0 0.0 copy-start
  0.0 1.2 %copy-done = bf16[64,8192]{1,0:T(8,128)(2,1)S(1)} copy-done((bf16[64,8192]{1,0:T(8,128)(2,1)S(1)}, bf16[64,8192]{1,0:T(8,128)(2,1)}, u32[]{:S(2)}) %copy-start) | copy-done | bytes 1048600
  1.2 0.0 copy-start.1
  1.2 0.9 %copy-done.1 = bf16[64,1024]{1,0:T(8,128)(2,1)S(1)} copy-done((bf16[64,1024]{1,0:T(8,128)(2,1)S(1)}, bf16[64,1024]{1,0:T(8,128)(2,1)}, u32[]{:S(2)}) %copy-start.1) | copy-done | bytes 131096
  2.1 0.0 copy-start.2
  2.1 0.9 %copy-done.2 = bf16[64,1024]{1,0:T(8,128)(2,1)S(1)} copy-done((bf16[64,1024]{1,0:T(8,128)(2,1)S(1)}, bf16[64,1024]{1,0:T(8,128)(2,1)}, u32[]{:S(2)}) %copy-start.2) | copy-done | bytes 131096
  3.0 0.0 copy-start.3
  3.0 0.7 %copy-done.3 = s32[6]{0:T(128)S(1)} copy-done((s32[6]{0:T(128)S(1)}, s32[6]{0:T(128)}, u32[]{:S(2)}) %copy-start.3) | copy-done | bytes 48
  3.7 0.0 copy-start.4
  3.7 0.7 %copy-done.4 = s32[16]{0:T(128)S(1)} copy-done((s32[16]{0:T(128)S(1)}, s32[16]{0:T(128)}, u32[]{:S(2)}) %copy-start.4) | copy-done | bytes 88
  4.3 56.3 %shard_map.55 = bf16[64,8192]{1,0:T(8,128)(2,1)S(1)} custom-call(s32[6]{0:T(128)S(1)} %copy-done.3, s32[16]{0:T(128)S(1)} %copy-done.4, bf16[64,8192]{1,0:T(8,128)(2,1)S(1)} %copy-done, bf16[64,1024]{1,0:T(8,128)(2,1)S(1)} %copy-done.1, bf16[64,1024]{1,0:T(8,128)(2,1)S(1)} %copy-done.2), custom_call_target="tpu_custom_call" | custom-call | tf_op jit(solution)/shard_map/pallas_call | solution.py:314
  60.7 1.0 %copy.7 = bf16[64,8192]{1,0:T(8,128)(2,1)} copy(bf16[64,8192]{1,0:T(8,128)(2,1)S(1)} %shard_map.55) | data formatting | bytes 2097152
Async XLA Ops:
  0.0 1.2 %copy-start = (bf16[64,8192]{1,0:T(8,128)(2,1)S(1)}, bf16[64,8192]{1,0:T(8,128)(2,1)}, u32[]{:S(2)}) copy-start(bf16[64,8192]{1,0:T(8,128)(2,1)} %q_hbm.1) | copy-start | bytes 3145732
  1.2 0.9 %copy-start.1 = (bf16[64,1024]{1,0:T(8,128)(2,1)S(1)}, bf16[64,1024]{1,0:T(8,128)(2,1)}, u32[]{:S(2)}) copy-start(bf16[64,1024]{1,0:T(8,128)(2,1)} %k_hbm.1) | copy-start | bytes 393220
  2.1 0.9 %copy-start.2 = (bf16[64,1024]{1,0:T(8,128)(2,1)S(1)}, bf16[64,1024]{1,0:T(8,128)(2,1)}, u32[]{:S(2)}) copy-start(bf16[64,1024]{1,0:T(8,128)(2,1)} %v_hbm.1) | copy-start | bytes 393220
  3.0 0.7 %copy-start.3 = (s32[6]{0:T(128)S(1)}, s32[6]{0:T(128)}, u32[]{:S(2)}) copy-start(s32[6]{0:T(128)} %lengths_ref.1) | copy-start | bytes 76
  3.7 0.7 %copy-start.4 = (s32[16]{0:T(128)S(1)}, s32[16]{0:T(128)}, u32[]{:S(2)}) copy-start(s32[16]{0:T(128)} %order_ref.1) | copy-start | bytes 196

commit v2 on v1

--- a/solution.py
+++ b/solution.py
@@ -30,16 +30,15 @@
     return pos, begin
 
 
-def fill_bias(bias_ref, order_ref, first_slot, pos, begin, block_length):
-    for j in range(bias_ref.shape[0] // block_length):
-        key = (
-            order_ref[first_slot + j] * block_length
-            + lax.broadcasted_iota(jnp.int32, (block_length, LANES), 0)
-        )
-        allowed = (key <= pos) & (key >= begin)
-        bias_ref[j * block_length : (j + 1) * block_length, :] = jnp.where(
-            allowed, 0.0, MASKED
-        ).astype(F32)
+def fill_bias(bias_ref, j, order_ref, slot, pos, begin, block_length):
+    key = (
+        order_ref[slot] * block_length
+        + lax.broadcasted_iota(jnp.int32, (block_length, LANES), 0)
+    )
+    allowed = (key <= pos) & (key >= begin)
+    bias_ref[j * block_length : (j + 1) * block_length, :] = jnp.where(
+        allowed, 0.0, MASKED
+    ).astype(F32)
 
 
 def stack_queries(g, q_ref, qt_ref, ratio):
@@ -53,7 +52,7 @@
 def attend(g, k, v, qt_ref, bias_ref, top_ref, total_ref, accum_ref):
     width = qt_ref.shape[2]
     scores = jnp.dot(k, qt_ref[g], preferred_element_type=F32)
-    scores = scores + jnp.concatenate([bias_ref[...]] * (width // LANES), axis=1)
+    scores = scores + jnp.concatenate([bias_ref[: k.shape[0]]] * (width // LANES), axis=1)
     top = top_ref[g]
     new_top = jnp.maximum(top, jnp.max(scores, axis=0, keepdims=True))
     weights = jnp.exp2((scores - new_top) * SCORE_TO_LOG2)
@@ -95,7 +94,9 @@
         pl.loop(0, groups)(lambda g: stack_queries(g, q_ref, qt_ref, ratio))
 
     pos, begin = query_limits(lengths_ref, order_ref, first_ref[0], rows, block_length)
-    fill_bias(bias_ref, order_ref, step * (chunk // block_length), pos, begin, block_length)
+    slots = chunk // block_length
+    for j in range(slots):
+        fill_bias(bias_ref, j, order_ref, step * slots + j, pos, begin, block_length)
 
     @pl.loop(0, groups)
     def _(g):
@@ -107,8 +108,8 @@
         pl.loop(0, groups)(lambda g: finish(g, out_ref, total_ref, accum_ref, rows, ratio))
 
 
-def gather_kernel(ratio, block_length, lengths_ref, order_ref, q_hbm, k_hbm, v_hbm, out_ref,
-                  q_ref, k_buf, v_buf, qt_ref, bias_ref, top_ref, total_ref, accum_ref,
+def gather_kernel(ratio, block_length, lengths_hbm, order_hbm, q_hbm, k_hbm, v_hbm, out_ref,
+                  lengths_ref, order_ref, q_ref, k_buf, v_buf, qt_ref, bias_ref, top_ref, total_ref, accum_ref,
                   local_sem, k_recv, v_recv, k_send, v_send):
     rows, width = k_hbm.shape
     groups = width // HEAD_WIDTH
@@ -156,6 +157,10 @@
     own_k.start()
     own_v.start()
     own_q.start()
+    own_lengths = pltpu.make_async_copy(lengths_hbm, lengths_ref, local_sem.at[3])
+    own_order = pltpu.make_async_copy(order_hbm, order_ref, local_sem.at[4])
+    own_lengths.start()
+    own_order.start()
     pl.semaphore_wait(barrier, 4 + zz)
 
     K = (k_hbm, k_buf, k_recv, k_send)
@@ -172,9 +177,9 @@
     def arrived(which, d):
         copy(which, d, SIB, sibling).wait_recv()
 
-    def up_down(which, i, d, wait=False):
+    def up_down(which, i, d, wait=False, own=False):
         def go(way, f):
-            one = copy(which, d, way, z_side(f), own=i == 0)
+            one = copy(which, d, way, z_side(f), own=own)
             one.wait_send() if wait else one.start()
 
         if i == 0:
@@ -190,18 +195,33 @@
             else:
                 go(ZU if i == 1 else ZD, 2 if i == 1 else 0)
 
+    def relay(i, dy, dx):
+        @pl.when(zz == 1)
+        def _():
+            d = shard(plane(i), dy, dx)
+            for which in (K, V):
+                arrived(which, d)
+                copy(which, d, ZD, z_side(0)).start()
+
+    def arrived_unless_relayed(which, d):
+        @pl.when(zz == 0)
+        def _():
+            arrived(which, d)
+
     def first(i):
-        p = plane(i)
-        a = shard(p, 0, 0)
+        a = shard(plane(i), 0, 0)
         own = i == 0
+        meet = arrived if i == 1 else arrived_unless_relayed
         if not own:
-            arrived(K, a)
+            meet(K, a)
         copy(K, a, YS, y_side, own).start()
-        up_down(K, i, a)
+        if i < 2:
+            up_down(K, i, a, own=own)
         if not own:
-            arrived(V, a)
+            meet(V, a)
         copy(V, a, XS, x_side, own).start()
-        up_down(V, i, a)
+        if i < 2:
+            up_down(V, i, a, own=own)
         copy(K, a, XS, x_side, own).start()
         copy(V, a, YS, y_side, own).start()
         copy(K, a, SIB, sibling, own).start()
@@ -211,9 +231,11 @@
         p = plane(i)
         b, d = shard(p, 1, 0), shard(p, 0, 1)
         arrived(K, b)
-        copy(K, b, XS, x_side).start()
+        if i in (0, 3):
+            copy(K, b, XS, x_side).start()
         arrived(V, d)
-        copy(V, d, YS, y_side).start()
+        if i in (0, 3):
+            copy(V, d, YS, y_side).start()
         copy(K, b, SIB, sibling).start()
         copy(V, d, SIB, sibling).start()
 
@@ -226,60 +248,78 @@
         copy(V, v_d, SIB, sibling).start()
 
     def fourth(i):
-        p = plane(i)
-        d = shard(p, 1, 1)
-        arrived(K, d)
-        copy(K, d, SIB, sibling).start()
-        arrived(V, d)
-        copy(V, d, SIB, sibling).start()
-
-    def from_sibling(i):
-        p = plane(i)
-        for dy, dx in ((0, 0), (1, 0), (0, 1), (1, 1)):
-            arrived(K, shard(p, dy, dx, 1))
-            arrived(V, shard(p, dy, dx, 1))
-
-    pos, begin = query_limits(lengths_ref, order_ref, me * rows, rows, block_length)
-    slots = 8 * rows // block_length
-
-    def prepare(i):
-        fill_bias(bias_ref, order_ref, plane(i) * slots, pos, begin, block_length)
-
-    def compute(i, lo, hi_):
-        p = plane(i)
+        d = shard(plane(i), 1, 1)
+        for which in (K, V):
+            (arrived_unless_relayed if i == 2 else arrived)(which, d)
+            if i == 0:
+                up_down(which, i, d)
+        for which in (K, V):
+            copy(which, d, SIB, sibling).start()
+
+    def from_sibling(chunk):
+        for i, dy, dx in chunk:
+            arrived(K, shard(plane(i), dy, dx, 1))
+            arrived(V, shard(plane(i), dy, dx, 1))
+
+    def prepare(chunk):
+        for j, (i, dy, dx) in enumerate(chunk):
+            fill_bias(bias_ref, j, order_ref, shard(plane(i), dy, dx) // 2, pos, begin,
+                      block_length)
+
+    def compute(chunk, lo, hi_, last=False):
+        pairs = [shard(plane(i), dy, dx) // 2 * 2 for i, dy, dx in chunk]
 
         @pl.loop(lo, hi_)
         def _(g):
-            k = k_buf[pl.ds(p * 8, 8), :, head_columns(g)].reshape(8 * rows, HEAD_WIDTH)
-            v = v_buf[pl.ds(p * 8, 8), :, head_columns(g)].reshape(8 * rows, HEAD_WIDTH)
+            k, v = (
+                jnp.concatenate([
+                    buf[pl.ds(d, 2), :, head_columns(g)].reshape(2 * rows, HEAD_WIDTH)
+                    for d in pairs
+                ], axis=0)
+                for buf in (k_buf, v_buf)
+            )
             attend(g, k, v, qt_ref, bias_ref, top_ref, total_ref, accum_ref)
-            if i == 3:
+            if last:
                 finish(g, out_ref, total_ref, accum_ref, rows, ratio)
 
+    def near(i):
+        return [(i, 0, 0), (i, 1, 0), (i, 0, 1)]
+
+    def far(i):
+        return [(i, 1, 1)]
+
     first(0)
+    own_lengths.wait()
+    own_order.wait()
+    pos, begin = query_limits(lengths_ref, order_ref, me * rows, rows, block_length)
     reset(top_ref, total_ref, accum_ref)
     own_q.wait()
     pl.loop(0, groups)(lambda g: stack_queries(g, q_ref, qt_ref, ratio))
     second(0)
     first(1)
+    relay(2, 0, 0)
     third(0)
     fourth(0)
     own_k.wait()
     own_v.wait()
-    for i in range(4):
-        from_sibling(i)
-        prepare(i)
-        if i < 3:
-            compute(i, 0, 2)
-            second(i + 1)
-            compute(i, 2, 4)
-            if i < 2:
-                first(i + 2)
-            third(i + 1)
-            compute(i, 4, groups)
-            fourth(i + 1)
-        else:
-            compute(i, 0, groups)
+    go = functools.partial
+    steps = [
+        (near(0) + far(0), [go(second, 1), go(first, 2), go(relay, 3, 0, 0), go(third, 1)]),
+        (near(1), [go(second, 2), go(first, 3), go(relay, 2, 1, 1), go(third, 2)]),
+        (near(2), [go(second, 3), go(fourth, 1), go(third, 3)]),
+        (near(3) + far(1), [go(fourth, 2), go(fourth, 3)]),
+        (far(2) + far(3), []),
+    ]
+    for n, (chunk, events) in enumerate(steps):
+        from_sibling(chunk)
+        prepare(chunk)
+        done = 0
+        for event in events:
+            compute(chunk, done, done + 2)
+            done += 2
+            event()
+        if done < groups:
+            compute(chunk, done, groups, last=n == len(steps) - 1)
 
     for i in range(4):
         p = plane(i)
@@ -287,8 +327,11 @@
         for which, extra in ((K, (b, XS, x_side)), (V, (d, YS, y_side))):
             copy(which, a, XS, x_side).wait_send()
             copy(which, a, YS, y_side).wait_send()
-            copy(which, *extra).wait_send()
+            if i in (0, 3):
+                copy(which, *extra).wait_send()
             up_down(which, i, a, wait=True)
+            if i in (0, 2):
+                up_down(which, i, e, wait=True)
             for s in (a, b, d, e):
                 copy(which, s, SIB, sibling).wait_send()
 
@@ -314,10 +357,12 @@
         return pl.pallas_call(
             functools.partial(gather_kernel, ratio, block_length),
             out_shape=out_shape,
-            in_specs=[smem, smem] + [pl.BlockSpec(memory_space=pl.ANY)] * 3,
+            in_specs=[pl.BlockSpec(memory_space=pltpu.HBM)] * 5,
             out_specs=pl.BlockSpec(memory_space=pltpu.VMEM),
-            scratch_shapes=[pltpu.VMEM(queries.shape, BF16), gathered, gathered] + scratch + [
-                pltpu.SemaphoreType.DMA((3,)),
+            scratch_shapes=[pltpu.SMEM(doc_lengths.shape, jnp.int32),
+                            pltpu.SMEM(stored_block_order.shape, jnp.int32),
+                            pltpu.VMEM(queries.shape, BF16), gathered, gathered] + scratch + [
+                pltpu.SemaphoreType.DMA((5,)),
                 pltpu.SemaphoreType.DMA((devices,)),
                 pltpu.SemaphoreType.DMA((devices,)),
                 pltpu.SemaphoreType.DMA((5, devices // 2)),

time: 61.9 us -> 55.9 us (0.903)
  Pallas kernels: 56.3 us -> 50.3 us
    pallas_call x1, Pallas kernels: 56.3 us -> 50.3 us  [body(): pl.pallas_call(functools.partial(gather_kernel, ratio, block_length), out...]
where the time goes in v2:
time: 55.9 us; the launch traced here: 55.7 us
  Pallas kernels  50.3 us (90%)
  local copies, waits for them, and re-layouts  5.31 us (9%)
    pallas_call x1, Pallas kernels, body(): pl.pallas_call(functools.partial(gather_kernel, ratio, block_length), out...  50.3 us
    unnamed x11, local copies, waits for them, and re-layouts  5.31 us

profile of v2, /device:TPU:0, one launch (start us, length us, event | category | flops | bytes accessed | tf_op | source)
XLA Modules:
  0.0 55.7 jit_solution(5702508643671032767)
XLA Ops:
  0.0 0.0 copy-start
  0.0 1.2 %copy-done = bf16[64,8192]{1,0:T(8,128)(2,1)S(1)} copy-done((bf16[64,8192]{1,0:T(8,128)(2,1)S(1)}, bf16[64,8192]{1,0:T(8,128)(2,1)}, u32[]{:S(2)}) %copy-start) | copy-done | bytes 1048600
  1.2 0.0 copy-start.1
  1.2 0.9 %copy-done.1 = bf16[64,1024]{1,0:T(8,128)(2,1)S(1)} copy-done((bf16[64,1024]{1,0:T(8,128)(2,1)S(1)}, bf16[64,1024]{1,0:T(8,128)(2,1)}, u32[]{:S(2)}) %copy-start.1) | copy-done | bytes 131096
  2.1 0.0 copy-start.2
  2.1 0.9 %copy-done.2 = bf16[64,1024]{1,0:T(8,128)(2,1)S(1)} copy-done((bf16[64,1024]{1,0:T(8,128)(2,1)S(1)}, bf16[64,1024]{1,0:T(8,128)(2,1)}, u32[]{:S(2)}) %copy-start.2) | copy-done | bytes 131096
  3.0 0.0 copy-start.3
  3.0 0.7 %copy-done.3 = s32[6]{0:T(128)S(1)} copy-done((s32[6]{0:T(128)S(1)}, s32[6]{0:T(128)}, u32[]{:S(2)}) %copy-start.3) | copy-done | bytes 48
  3.7 0.0 copy-start.4
  3.7 0.7 %copy-done.4 = s32[16]{0:T(128)S(1)} copy-done((s32[16]{0:T(128)S(1)}, s32[16]{0:T(128)}, u32[]{:S(2)}) %copy-start.4) | copy-done | bytes 88
  4.3 50.3 %shard_map.55 = bf16[64,8192]{1,0:T(8,128)(2,1)S(1)} custom-call(s32[6]{0:T(128)S(1)} %copy-done.3, s32[16]{0:T(128)S(1)} %copy-done.4, bf16[64,8192]{1,0:T(8,128)(2,1)S(1)} %copy-done, bf16[64,1024]{1,0:T(8,128)(2,1)S(1)} %copy-done.1, bf16[64,1024]{1,0:T(8,128)(2,1)S(1)} %copy-done.2), custom_call_target="tpu_custom_call" | custom-call | tf_op jit(solution)/shard_map/pallas_call | solution.py:357
  54.7 1.0 %copy.7 = bf16[64,8192]{1,0:T(8,128)(2,1)} copy(bf16[64,8192]{1,0:T(8,128)(2,1)S(1)} %shard_map.55) | data formatting | bytes 2097152
Async XLA Ops:
  0.0 1.2 %copy-start = (bf16[64,8192]{1,0:T(8,128)(2,1)S(1)}, bf16[64,8192]{1,0:T(8,128)(2,1)}, u32[]{:S(2)}) copy-start(bf16[64,8192]{1,0:T(8,128)(2,1)} %q_hbm.1) | copy-start | bytes 3145732
  1.2 0.9 %copy-start.1 = (bf16[64,1024]{1,0:T(8,128)(2,1)S(1)}, bf16[64,1024]{1,0:T(8,128)(2,1)}, u32[]{:S(2)}) copy-start(bf16[64,1024]{1,0:T(8,128)(2,1)} %k_hbm.1) | copy-start | bytes 393220
  2.1 0.9 %copy-start.2 = (bf16[64,1024]{1,0:T(8,128)(2,1)S(1)}, bf16[64,1024]{1,0:T(8,128)(2,1)}, u32[]{:S(2)}) copy-start(bf16[64,1024]{1,0:T(8,128)(2,1)} %v_hbm.1) | copy-start | bytes 393220
  3.0 0.7 %copy-start.3 = (s32[6]{0:T(128)S(1)}, s32[6]{0:T(128)}, u32[]{:S(2)}) copy-start(s32[6]{0:T(128)} %lengths_hbm.1) | copy-start | bytes 76
  3.7 0.7 %copy-start.4 = (s32[16]{0:T(128)S(1)}, s32[16]{0:T(128)}, u32[]{:S(2)}) copy-start(s32[16]{0:T(128)} %order_hbm.1) | copy-start | bytes 196

commit v3 on v2

--- a/solution.py
+++ b/solution.py
@@ -49,19 +49,26 @@
     qt_ref[g] = jnp.concatenate(heads, axis=0).T
 
 
-def attend(g, k, v, qt_ref, bias_ref, top_ref, total_ref, accum_ref):
+def attend(gs, ks, vs, qt_ref, bias_ref, top_ref, total_ref, accum_ref):
     width = qt_ref.shape[2]
-    scores = jnp.dot(k, qt_ref[g], preferred_element_type=F32)
-    scores = scores + jnp.concatenate([bias_ref[: k.shape[0]]] * (width // LANES), axis=1)
-    top = top_ref[g]
-    new_top = jnp.maximum(top, jnp.max(scores, axis=0, keepdims=True))
-    weights = jnp.exp2((scores - new_top) * SCORE_TO_LOG2)
-    factor = jnp.exp2((top - new_top) * SCORE_TO_LOG2)
-    top_ref[g] = new_top
-    total_ref[g] = total_ref[g] * factor + jnp.sum(weights, axis=0, keepdims=True)
-    accum_ref[g] = accum_ref[g] * factor + jnp.dot(
-        v.T, weights.astype(BF16), preferred_element_type=F32
-    )
+    bias = jnp.concatenate([bias_ref[: ks[0].shape[0]]] * (width // LANES), axis=1)
+    states = [(top_ref[g], total_ref[g], accum_ref[g]) for g in gs]
+    scores = [jnp.dot(k, qt_ref[g], preferred_element_type=F32) for g, k in zip(gs, ks)]
+    results = []
+    for (top, total, accum), s, v in zip(states, scores, vs):
+        s = s + bias
+        new_top = jnp.maximum(top, jnp.max(s, axis=0, keepdims=True))
+        weights = jnp.exp2((s - new_top) * SCORE_TO_LOG2)
+        factor = jnp.exp2((top - new_top) * SCORE_TO_LOG2)
+        total = total * factor + jnp.sum(weights, axis=0, keepdims=True)
+        accum = accum * factor + jnp.dot(
+            v.T, weights.astype(BF16), preferred_element_type=F32
+        )
+        results.append((new_top, total, accum))
+    for g, (top, total, accum) in zip(gs, results):
+        top_ref[g] = top
+        total_ref[g] = total
+        accum_ref[g] = accum
 
 
 def finish(g, out_ref, total_ref, accum_ref, rows, ratio):
@@ -100,7 +107,7 @@
 
     @pl.loop(0, groups)
     def _(g):
-        attend(g, k_ref[:, head_columns(g)], v_ref[:, head_columns(g)],
+        attend([g], [k_ref[:, head_columns(g)]], [v_ref[:, head_columns(g)]],
                qt_ref, bias_ref, top_ref, total_ref, accum_ref)
 
     @pl.when(step == pl.num_programs(0) - 1)
@@ -269,18 +276,20 @@
     def compute(chunk, lo, hi_, last=False):
         pairs = [shard(plane(i), dy, dx) // 2 * 2 for i, dy, dx in chunk]
 
-        @pl.loop(lo, hi_)
-        def _(g):
-            k, v = (
-                jnp.concatenate([
-                    buf[pl.ds(d, 2), :, head_columns(g)].reshape(2 * rows, HEAD_WIDTH)
-                    for d in pairs
-                ], axis=0)
-                for buf in (k_buf, v_buf)
-            )
-            attend(g, k, v, qt_ref, bias_ref, top_ref, total_ref, accum_ref)
+        def load(buf, g):
+            return jnp.concatenate([
+                buf[pl.ds(d, 2), :, head_columns(g)].reshape(2 * rows, HEAD_WIDTH)
+                for d in pairs
+            ], axis=0)
+
+        @pl.loop(lo, hi_, step=2)
+        def _(first_g):
+            gs = [first_g + j for j in range(2)]
+            attend(gs, [load(k_buf, g) for g in gs], [load(v_buf, g) for g in gs],
+                   qt_ref, bias_ref, top_ref, total_ref, accum_ref)
             if last:
-                finish(g, out_ref, total_ref, accum_ref, rows, ratio)
+                for g in gs:
+                    finish(g, out_ref, total_ref, accum_ref, rows, ratio)
 
     def near(i):
         return [(i, 0, 0), (i, 1, 0), (i, 0, 1)]

time: 55.9 us -> 53.2 us (0.952)
  Pallas kernels: 50.3 us -> 47.7 us
    pallas_call x1, Pallas kernels: 50.3 us -> 47.7 us  [body(): pl.pallas_call(functools.partial(gather_kernel, ratio, block_length), out...]
where the time goes in v3:
time: 53.2 us; the launch traced here: 53 us
  Pallas kernels  47.7 us (90%)
  local copies, waits for them, and re-layouts  5.31 us (10%)
    pallas_call x1, Pallas kernels, body(): pl.pallas_call(functools.partial(gather_kernel, ratio, block_length), out...  47.7 us
    unnamed x11, local copies, waits for them, and re-layouts  5.31 us

profile of v3, /device:TPU:0, one launch (start us, length us, event | category | flops | bytes accessed | tf_op | source)
XLA Modules:
  0.0 53.0 jit_solution(3933460513636730778)
XLA Ops:
  0.0 0.0 copy-start
  0.0 1.2 %copy-done = bf16[64,8192]{1,0:T(8,128)(2,1)S(1)} copy-done((bf16[64,8192]{1,0:T(8,128)(2,1)S(1)}, bf16[64,8192]{1,0:T(8,128)(2,1)}, u32[]{:S(2)}) %copy-start) | copy-done | bytes 1048600
  1.2 0.0 copy-start.1
  1.2 0.9 %copy-done.1 = bf16[64,1024]{1,0:T(8,128)(2,1)S(1)} copy-done((bf16[64,1024]{1,0:T(8,128)(2,1)S(1)}, bf16[64,1024]{1,0:T(8,128)(2,1)}, u32[]{:S(2)}) %copy-start.1) | copy-done | bytes 131096
  2.1 0.0 copy-start.2
  2.1 0.9 %copy-done.2 = bf16[64,1024]{1,0:T(8,128)(2,1)S(1)} copy-done((bf16[64,1024]{1,0:T(8,128)(2,1)S(1)}, bf16[64,1024]{1,0:T(8,128)(2,1)}, u32[]{:S(2)}) %copy-start.2) | copy-done | bytes 131096
  3.0 0.0 copy-start.3
  3.0 0.7 %copy-done.3 = s32[6]{0:T(128)S(1)} copy-done((s32[6]{0:T(128)S(1)}, s32[6]{0:T(128)}, u32[]{:S(2)}) %copy-start.3) | copy-done | bytes 48
  3.7 0.0 copy-start.4
  3.7 0.7 %copy-done.4 = s32[16]{0:T(128)S(1)} copy-done((s32[16]{0:T(128)S(1)}, s32[16]{0:T(128)}, u32[]{:S(2)}) %copy-start.4) | copy-done | bytes 88
  4.3 47.7 %shard_map.55 = bf16[64,8192]{1,0:T(8,128)(2,1)S(1)} custom-call(s32[6]{0:T(128)S(1)} %copy-done.3, s32[16]{0:T(128)S(1)} %copy-done.4, bf16[64,8192]{1,0:T(8,128)(2,1)S(1)} %copy-done, bf16[64,1024]{1,0:T(8,128)(2,1)S(1)} %copy-done.1, bf16[64,1024]{1,0:T(8,128)(2,1)S(1)} %copy-done.2), custom_call_target="tpu_custom_call" | custom-call | tf_op jit(solution)/shard_map/pallas_call | solution.py:366
  52.1 1.0 %copy.7 = bf16[64,8192]{1,0:T(8,128)(2,1)} copy(bf16[64,8192]{1,0:T(8,128)(2,1)S(1)} %shard_map.55) | data formatting | bytes 2097152
Async XLA Ops:
  0.0 1.2 %copy-start = (bf16[64,8192]{1,0:T(8,128)(2,1)S(1)}, bf16[64,8192]{1,0:T(8,128)(2,1)}, u32[]{:S(2)}) copy-start(bf16[64,8192]{1,0:T(8,128)(2,1)} %q_hbm.1) | copy-start | bytes 3145732
  1.2 0.9 %copy-start.1 = (bf16[64,1024]{1,0:T(8,128)(2,1)S(1)}, bf16[64,1024]{1,0:T(8,128)(2,1)}, u32[]{:S(2)}) copy-start(bf16[64,1024]{1,0:T(8,128)(2,1)} %k_hbm.1) | copy-start | bytes 393220
  2.1 0.9 %copy-start.2 = (bf16[64,1024]{1,0:T(8,128)(2,1)S(1)}, bf16[64,1024]{1,0:T(8,128)(2,1)}, u32[]{:S(2)}) copy-start(bf16[64,1024]{1,0:T(8,128)(2,1)} %v_hbm.1) | copy-start | bytes 393220
  3.0 0.7 %copy-start.3 = (s32[6]{0:T(128)S(1)}, s32[6]{0:T(128)}, u32[]{:S(2)}) copy-start(s32[6]{0:T(128)} %lengths_hbm.1) | copy-start | bytes 76
  3.7 0.7 %copy-start.4 = (s32[16]{0:T(128)S(1)}, s32[16]{0:T(128)}, u32[]{:S(2)}) copy-start(s32[16]{0:T(128)} %order_hbm.1) | copy-start | bytes 196

commit v4 on v3

--- a/solution.py
+++ b/solution.py
@@ -60,10 +60,9 @@
         new_top = jnp.maximum(top, jnp.max(s, axis=0, keepdims=True))
         weights = jnp.exp2((s - new_top) * SCORE_TO_LOG2)
         factor = jnp.exp2((top - new_top) * SCORE_TO_LOG2)
-        total = total * factor + jnp.sum(weights, axis=0, keepdims=True)
-        accum = accum * factor + jnp.dot(
-            v.T, weights.astype(BF16), preferred_element_type=F32
-        )
+        both = jnp.dot(jnp.concatenate([v.T, jnp.ones((16, v.shape[0]), BF16)], axis=0), weights.astype(BF16), preferred_element_type=F32)
+        accum = accum * factor + both[:HEAD_WIDTH]
+        total = total * factor + both[HEAD_WIDTH:HEAD_WIDTH + 1]
         results.append((new_top, total, accum))
     for g, (top, total, accum) in zip(gs, results):
         top_ref[g] = top

time: 53.2 us -> 52.8 us (level)
  no operation moved by 1% of the time
where the time goes in v4:
time: 52.8 us; the launch traced here: 52.6 us
  Pallas kernels  47.2 us (89%)
  local copies, waits for them, and re-layouts  5.31 us (10%)
    pallas_call x1, Pallas kernels, body(): pl.pallas_call(functools.partial(gather_kernel, ratio, block_length), out...  47.2 us
    unnamed x11, local copies, waits for them, and re-layouts  5.31 us

profile of v4, /device:TPU:0, one launch (start us, length us, event | category | flops | bytes accessed | tf_op | source)
XLA Modules:
  0.0 52.6 jit_solution(2500787977340828563)
XLA Ops:
  0.0 0.0 copy-start
  0.0 1.2 %copy-done = bf16[64,8192]{1,0:T(8,128)(2,1)S(1)} copy-done((bf16[64,8192]{1,0:T(8,128)(2,1)S(1)}, bf16[64,8192]{1,0:T(8,128)(2,1)}, u32[]{:S(2)}) %copy-start) | copy-done | bytes 1048600
  1.2 0.0 copy-start.1
  1.2 0.9 %copy-done.1 = bf16[64,1024]{1,0:T(8,128)(2,1)S(1)} copy-done((bf16[64,1024]{1,0:T(8,128)(2,1)S(1)}, bf16[64,1024]{1,0:T(8,128)(2,1)}, u32[]{:S(2)}) %copy-start.1) | copy-done | bytes 131096
  2.1 0.0 copy-start.2
  2.1 0.9 %copy-done.2 = bf16[64,1024]{1,0:T(8,128)(2,1)S(1)} copy-done((bf16[64,1024]{1,0:T(8,128)(2,1)S(1)}, bf16[64,1024]{1,0:T(8,128)(2,1)}, u32[]{:S(2)}) %copy-start.2) | copy-done | bytes 131096
  3.0 0.0 copy-start.3
  3.0 0.7 %copy-done.3 = s32[6]{0:T(128)S(1)} copy-done((s32[6]{0:T(128)S(1)}, s32[6]{0:T(128)}, u32[]{:S(2)}) %copy-start.3) | copy-done | bytes 48
  3.7 0.0 copy-start.4
  3.7 0.7 %copy-done.4 = s32[16]{0:T(128)S(1)} copy-done((s32[16]{0:T(128)S(1)}, s32[16]{0:T(128)}, u32[]{:S(2)}) %copy-start.4) | copy-done | bytes 88
  4.3 47.2 %shard_map.55 = bf16[64,8192]{1,0:T(8,128)(2,1)S(1)} custom-call(s32[6]{0:T(128)S(1)} %copy-done.3, s32[16]{0:T(128)S(1)} %copy-done.4, bf16[64,8192]{1,0:T(8,128)(2,1)S(1)} %copy-done, bf16[64,1024]{1,0:T(8,128)(2,1)S(1)} %copy-done.1, bf16[64,1024]{1,0:T(8,128)(2,1)S(1)} %copy-done.2), custom_call_target="tpu_custom_call" | custom-call | tf_op jit(solution)/shard_map/pallas_call | solution.py:365
  51.6 1.0 %copy.7 = bf16[64,8192]{1,0:T(8,128)(2,1)} copy(bf16[64,8192]{1,0:T(8,128)(2,1)S(1)} %shard_map.55) | data formatting | bytes 2097152
Async XLA Ops:
  0.0 1.2 %copy-start = (bf16[64,8192]{1,0:T(8,128)(2,1)S(1)}, bf16[64,8192]{1,0:T(8,128)(2,1)}, u32[]{:S(2)}) copy-start(bf16[64,8192]{1,0:T(8,128)(2,1)} %q_hbm.1) | copy-start | bytes 3145732
  1.2 0.9 %copy-start.1 = (bf16[64,1024]{1,0:T(8,128)(2,1)S(1)}, bf16[64,1024]{1,0:T(8,128)(2,1)}, u32[]{:S(2)}) copy-start(bf16[64,1024]{1,0:T(8,128)(2,1)} %k_hbm.1) | copy-start | bytes 393220
  2.1 0.9 %copy-start.2 = (bf16[64,1024]{1,0:T(8,128)(2,1)S(1)}, bf16[64,1024]{1,0:T(8,128)(2,1)}, u32[]{:S(2)}) copy-start(bf16[64,1024]{1,0:T(8,128)(2,1)} %v_hbm.1) | copy-start | bytes 393220
  3.0 0.7 %copy-start.3 = (s32[6]{0:T(128)S(1)}, s32[6]{0:T(128)}, u32[]{:S(2)}) copy-start(s32[6]{0:T(128)} %lengths_hbm.1) | copy-start | bytes 76
  3.7 0.7 %copy-start.4 = (s32[16]{0:T(128)S(1)}, s32[16]{0:T(128)}, u32[]{:S(2)}) copy-start(s32[16]{0:T(128)} %order_hbm.1) | copy-start | bytes 196
